TPU v7x, 512 devices: a whole 4x4x16 slice. The times are simulated.
512 devices in a mesh: dp: 4 (over x), expert: 8 (over y, core), shard: 16 (over z).
Axes of the slice: x: 4, y: 4, z: 16, core: 2. Of those that a mesh axis runs over, the one named last changes fastest.
Arguments:
- output_gradient: bfloat16 [65536, 3072], P(('dp', 'expert', 'shard')), may hold values from -24 to 24
- saved_router_scores: float32 [65536, 8], P(('dp', 'expert', 'shard')), may hold values from -8 to 8
- expert_choice_index: int32 [65536, 2], P(('dp', 'expert', 'shard')), may hold values from 0 to 7, as said below
- router_matrix: bfloat16 [8, 3072], replicated, may hold values from -0.109375 to 0.109375
- weight_normalized_entries: bfloat16 [3072, 8192], P('shard', 'expert'), may hold values from -1 to 1
- scales: bfloat16 [48, 8192], P('shard', 'expert'), may hold values from 0.0099487305 to 0.099609375
- stored_hidden_state: bfloat16 [4, 16, 256, 8192], P('dp', 'shard', None, 'expert'), may hold values from -6 to 6
- context: bfloat16 [65536, 3072], P(('dp', 'expert', 'shard')), may hold values from -6 to 6
- adapter_down_factor: bfloat16 [64, 3072], replicated, may hold values from -0.109375 to 0.109375
- adapter_up_factor: bfloat16 [64, 3072], replicated, may hold values from -0.109375 to 0.109375
Outputs:
- hidden_grad: bfloat16 [4, 16, 256, 8192], P('dp', 'shard', None, 'expert')
- token_grad: bfloat16 [65536, 3072], P(('dp', 'expert', 'shard'))
- grad_down: float32 [64, 3072], P(None, 'shard')
- up_factor_gradient: float32 [64, 3072], P(None, 'shard')
Inputs may be any that keep to these rules, and one draw needn't show every extreme that they name: `expert_choice_index`: each token names two different experts and expert 0 at most once. The 128 tokens of one device block name expert 0 at most 32 times, and in every draw all device blocks of some pair of dp and shard indices name it exactly 32 times.
All inputs are finite; a program needn't handle non-finite values.
Results may differ from a plain program's by a relative error of at most 0.015.
Values may be sent and summed in bfloat16 or wider, within the bound.
A program may use at most 64 MiB of HBM per device.

v0:
```python
import jax
import jax.numpy as jnp
from jax import lax
from jax.sharding import PartitionSpec as P

ADAPTER_SCALE = 0.25


def per_device(
    output_gradient,
    saved_router_scores,
    expert_choice_index,
    router_matrix,
    weight_normalized_entries,
    scales,
    stored_hidden_state,
    context,
    adapter_down_factor,
    adapter_up_factor,
):
    expert_count = lax.axis_size("expert")
    shard_count = lax.axis_size("shard")
    tokens, feature_width = output_gradient.shape
    experts = saved_router_scores.shape[1]
    row_count = stored_hidden_state.shape[2]
    capacity = row_count // expert_count
    ff_share = stored_hidden_state.shape[3]
    block_size = weight_normalized_entries.shape[0] // scales.shape[0]
    labels = jnp.arange(experts, dtype=jnp.int32)
    choose = expert_choice_index[:, :, None] == labels[None, None, :]
    chosen = jnp.sum(jnp.where(choose, saved_router_scores[:, None, :], 0.0), axis=2)
    first_prob = 1.0 / (1.0 + jnp.exp(chosen[:, 1] - chosen[:, 0]))
    second_prob = 1.0 - first_prob
    in_window = expert_choice_index == 0
    window_flag = jnp.any(in_window, axis=1)
    flag_int = window_flag.astype(jnp.int32)
    slot_index = jnp.cumsum(flag_int) - flag_int
    route_probs = jnp.stack([first_prob, second_prob], axis=1).astype(jnp.bfloat16)
    window_prob = jnp.where(in_window[:, 0], route_probs[:, 0], route_probs[:, 1])
    slot_labels = jnp.arange(capacity, dtype=jnp.int32)
    placement = (window_flag[None, :] & (slot_index[None, :] == slot_labels[:, None])).astype(
        jnp.bfloat16
    )
    send_rows = jnp.dot(placement, output_gradient, preferred_element_type=jnp.float32).astype(
        jnp.bfloat16
    )
    send_probs = jnp.dot(placement, window_prob, preferred_element_type=jnp.float32).astype(
        jnp.bfloat16
    )
    all_rows, all_probs = (
        lax.all_gather(send_rows, "expert", axis=0, tiled=True),
        lax.all_gather(send_probs, "expert", axis=0, tiled=True),
    )
    code_blocks = weight_normalized_entries.reshape(scales.shape[0], block_size, ff_share)
    own_weight = (
        (code_blocks.astype(jnp.float32) * scales.astype(jnp.float32)[:, None, :])
        .astype(jnp.bfloat16)
        .reshape(weight_normalized_entries.shape[0], ff_share)
    )
    product = jnp.dot(
        all_rows,
        lax.all_gather(own_weight, "shard", axis=0, tiled=True),
        preferred_element_type=jnp.float32,
    )
    hidden_grad = (all_probs.astype(jnp.float32)[:, None] * product).astype(jnp.bfloat16)
    partial_value = jnp.sum(stored_hidden_state[0, 0].astype(jnp.float32) * product, axis=1)
    returned = lax.psum_scatter(partial_value, "expert", scatter_dimension=0, tiled=True)
    window_grad = jnp.where(window_flag, returned[jnp.minimum(slot_index, capacity - 1)], 0.0)
    pair_grad = jnp.where(in_window, window_grad[:, None], 0.0)
    spread = first_prob * second_prob * (pair_grad[:, 0] - pair_grad[:, 1])
    sign_table = choose[:, 0, :].astype(jnp.float32) - choose[:, 1, :].astype(jnp.float32)
    logit_grad = (spread[:, None] * sign_table).astype(jnp.bfloat16)
    token_grad = jnp.dot(logit_grad, router_matrix, preferred_element_type=jnp.float32).astype(
        jnp.bfloat16
    )
    token_kept = lax.optimization_barrier(token_grad)
    residual_gradient = (
        output_gradient.astype(jnp.float32) + token_kept.astype(jnp.float32)
    ).astype(jnp.bfloat16)
    narrow_input = lax.dot_general(
        context, adapter_down_factor, (((1,), (1,)), ((), ())), preferred_element_type=jnp.float32
    ).astype(jnp.bfloat16)
    narrow_gradient = (
        ADAPTER_SCALE
        * lax.dot_general(
            residual_gradient,
            adapter_up_factor,
            (((1,), (1,)), ((), ())),
            preferred_element_type=jnp.float32,
        )
    ).astype(jnp.bfloat16)
    partial_up_gradient = ADAPTER_SCALE * lax.dot_general(
        narrow_input,
        residual_gradient,
        (((0,), (0,)), ((), ())),
        preferred_element_type=jnp.float32,
    )
    part_down = lax.dot_general(
        narrow_gradient, context, (((0,), (0,)), ((), ())), preferred_element_type=jnp.float32
    )
    summed_up, summed_down = lax.psum((partial_up_gradient, part_down), ("dp", "expert", "shard"))
    share_width = feature_width // shard_count
    first_col = lax.axis_index("shard") * share_width
    up_factor_gradient = lax.dynamic_slice_in_dim(summed_up, first_col, share_width, 1)
    grad_down = lax.dynamic_slice_in_dim(summed_down, first_col, share_width, 1)
    return (
        hidden_grad.reshape(stored_hidden_state.shape),
        token_grad,
        grad_down,
        up_factor_gradient,
    )


def solution(mesh):
    in_specs = (
        P(("dp", "expert", "shard"), None),
        P(("dp", "expert", "shard"), None),
        P(("dp", "expert", "shard"), None),
        P(),
        P("shard", "expert"),
        P("shard", "expert"),
        P("dp", "shard", None, "expert"),
        P(("dp", "expert", "shard"), None),
        P(),
        P(),
    )
    out_specs = (
        P("dp", "shard", None, "expert"),
        P(("dp", "expert", "shard"), None),
        P(None, "shard"),
        P(None, "shard"),
    )
    return jax.shard_map(
        per_device, mesh=mesh, in_specs=in_specs, out_specs=out_specs, check_vma=False
    )
```

profile of v0, /device:TPU:2, one launch (start us, length us, event | category | flops | bytes accessed | tf_op | source)
XLA Modules:
  0.0 639.7 jit_solution(14666868364817851319)
XLA Ops:
  7.2 0.0 copy-start
  7.2 0.0 copy-start.7
  7.2 0.0 copy-start.5
  7.2 0.0 copy-start.3
  7.2 0.0 copy-start.6
  7.2 0.0 copy-start.8
  7.2 0.0 all-gather.3.cloned.1.call-start
  7.3 0.8 fusion.24
  8.1 0.1 copy.26
  8.2 0.2 reduce-window.4
  8.4 0.1 fusion.6
  8.5 2.0 convolution_convert_fusion.1
  10.6 0.0 all-gather.3.cloned.1.call-update
  10.6 0.0 all-gather.5.cloned.1.call-start
  10.6 0.7 convert_element_type.90
  11.3 0.0 copy-done.3
  11.3 0.8 fusion.4
  12.2 0.0 all-gather.5.cloned.1.call-update
  12.2 0.0 all-reduce.5.cloned.1.call-start
  12.3 0.0 copy-done.7
  12.3 0.6 fusion.25
  13.5 0.0 copy-done.5
  13.5 0.0 copy-done.6
  13.6 0.0 copy-start.4
  13.6 33.7 %all-gather.3.cloned.1.call-done = bf16[256,3072]{1,0:T(8,128)(2,1)} async-done(((bf16[32,3072]{1,0:T(8,128)(2,1)}), bf16[256,3072]{1,0:T(8,128)(2,1)}) %all-gather.3.cloned.1.call-update) | async-done | bytes 1572880 | tf_op jit(solution)/shard_map/all_gather | solution.py:51
  47.3 89.3 %all-gather.5.cloned.1.call-done = bf16[3072,1024]{1,0:T(8,128)(2,1)} async-done(((bf16[192,1024]{1,0:T(8,128)(2,1)}), bf16[3072,1024]{1,0:T(8,128)(2,1)}) %all-gather.5.cloned.1.call-update) | async-done | bytes 6291472 | tf_op jit(solution)/shard_map/all_gather | solution.py:62
  136.5 0.0 copy-done.8
  136.5 5.2 fusion.3
  141.7 0.0 copy-start.1
  141.7 12.6 %all-reduce.1 = f32[256]{0:T(256)S(1)} all-reduce(f32[256]{0:T(256)S(1)} %get-tuple-element.14), channel_id=2, replica_groups=mesh['dp'=4,'expert'=8,'shard'=16] {'expert'}, use_global_device_ids=true, to_apply=%region_4.5.clone | all-reduce | flops 256 | bytes 2048
  154.3 0.1 dynamic-slice.2
  154.3 1.2 gather_fusion
  155.6 0.0 copy-done.4
  155.6 0.4 convolution_convert_fusion
  156.0 0.0 copy-done
  156.1 0.0 copy-done.1
  156.1 0.0 copy-start.2
  156.1 3.0 convolution_multiply_fusion
  159.0 0.0 copy-done.2
  159.0 2.7 fusion.1
  161.7 0.0 all-reduce.5.cloned.1.call-update
  162.4 0.1 fusion.2
  162.5 0.2 dynamic-update-slice
  162.7 12.4 %all-reduce = bf16[256]{0:T(256)(128)(2,1)S(1)} all-reduce(bf16[256]{0:T(256)(128)(2,1)S(1)} %dynamic-update-slice), channel_id=1, replica_groups=mesh['dp'=4,'expert'=8,'shard'=16] {'expert'}, use_global_device_ids=true, to_apply=%add | all-reduce | flops 256 | bytes 1024
  175.1 0.9 fusion.5
  176.1 455.4 %all-reduce.5.cloned.1.call-done = (f32[64,3072]{1,0:T(8,128)}, f32[64,3072]{1,0:T(8,128)}) async-done(((f32[64,3072]{1,0:T(8,128)}, f32[64,3072]{1,0:T(8,128)}), (f32[64,3072]{1,0:T(8,128)}, f32[64,3072]{1,0:T(8,128)})) %all-reduce.5.cloned.1.call-update) | async-done | bytes 1572880 | tf_op jit(solution)/shard_map/psum | solution.py:101
  631.5 1.7 constant_dynamic-slice_fusion
  (10 shorter events, 0.1 us)
Async XLA Ops:
  7.2 148.9 %copy-start = (bf16[128,3072]{1,0:T(8,128)(2,1)S(1)}, bf16[128,3072]{1,0:T(8,128)(2,1)}, u32[]{:S(2)}) copy-start(bf16[128,3072]{1,0:T(8,128)(2,1)} %param.17) | copy-start | bytes 2359300
  7.2 5.1 copy-start.7
  7.2 6.3 copy-start.5
  7.2 4.1 copy-start.3
  7.2 6.3 copy-start.6
  7.2 129.3 %copy-start.8 = (bf16[1,1,256,1024]{3,2,1,0:T(8,128)(2,1)S(1)}, bf16[1,1,256,1024]{3,2,1,0:T(8,128)(2,1)}, u32[]{:S(2)}) copy-start(bf16[1,1,256,1024]{3,2,1,0:T(8,128)(2,1)} %param.16) | copy-start | bytes 1572868
  7.2 40.0 %all-gather.3.cloned.1.call-start = ((), (), s32[]{:S(2)}) async-start(), calls=%async_computation | async-start | bytes 1769472 | tf_op jit(solution)/shard_map/all_gather | solution.py:51
  10.6 125.9 %all-gather.5.cloned.1.call-start = ((), (), s32[]{:S(2)}) async-start(), calls=%async_computation.1 | async-start | bytes 6684672 | tf_op jit(solution)/shard_map/all_gather | solution.py:62
  12.2 619.3 %all-reduce.5.cloned.1.call-start = ((), (), s32[]{:S(2)}) async-start(), calls=%async_computation.2 | async-start | bytes 3145728 | tf_op jit(solution)/shard_map/psum | solution.py:101
  13.6 142.0 %copy-start.4 = (bf16[8,3072]{1,0:T(8,128)(2,1)S(1)}, bf16[8,3072]{1,0:T(8,128)(2,1)}, u32[]{:S(2)}) copy-start(bf16[8,3072]{1,0:T(8,128)(2,1)} %param.13) | copy-start | bytes 147460
  141.7 14.4 %copy-start.1 = (bf16[128,3072]{1,0:T(8,128)(2,1)S(1)}, bf16[128,3072]{1,0:T(8,128)(2,1)}, u32[]{:S(2)}) copy-start(bf16[128,3072]{1,0:T(8,128)(2,1)} %param.10) | copy-start | bytes 2359300
  156.1 3.0 copy-start.2
Sparse Core Ops, SparseCore 0:
  10.8 36.4 all-gather.2
  49.9 86.5 all-gather.4
  161.9 469.5 all-reduce.4
where the time goes:
time: 640 us
  waiting for transfers between devices  578 us (90%)
  blocking collectives  25 us (4%)
  between operations  15.2 us (2%)
  matrix products  13.4 us (2%)
    psum x1, waiting for transfers between devices, per_device(): lax.psum((partial_up_gradient, part_down), ('dp', 'expert', 'shard'))  455 us
    all_gather x1, waiting for transfers between devices, per_device(): lax.all_gather(own_weight, 'shard', axis=0, tiled=True)  89.3 us
    all_gather x1, waiting for transfers between devices, per_device(): lax.all_gather(send_rows, 'expert', axis=0, tiled=True)  33.7 us
    unnamed x2, blocking collectives  25 us
  transfers between devices with their start and end apart: 3, of which 3 were waited for; matrix products, arithmetic and copies ran while one was open for 1% of the time, Pallas kernels for 0%

commit v1 on v0

--- a/solution.py
+++ b/solution.py
@@ -98,7 +98,15 @@
     part_down = lax.dot_general(
         narrow_gradient, context, (((0,), (0,)), ((), ())), preferred_element_type=jnp.float32
     )
-    summed_up, summed_down = lax.psum((partial_up_gradient, part_down), ("dp", "expert", "shard"))
+
+    def change_view_on(mine_x, axis_key, net_axis):
+        for t in (axis_key, net_axis):
+            mine_x = lax.psum(mine_x, t)
+        return mine_x
+
+    summed_up, summed_down = change_view_on(
+        (partial_up_gradient, part_down), ("expert", "shard"), "dp"
+    )
     share_width = feature_width // shard_count
     first_col = lax.axis_index("shard") * share_width
     up_factor_gradient = lax.dynamic_slice_in_dim(summed_up, first_col, share_width, 1)

time: 640 us -> 579 us (0.905)
  the two profiles are of different devices: /device:TPU:2 before, /device:TPU:1 now
where the time goes in v1:
time: 579 us
  waiting for transfers between devices  513 us (89%)
  blocking collectives  29.2 us (5%)
  between operations  15.3 us (3%)
  matrix products  13.4 us (2%)
    psum x2, waiting for transfers between devices, change_view_on(): mine_x = lax.psum(mine_x, t)  392 us
    all_gather x1, waiting for transfers between devices, per_device(): lax.all_gather(own_weight, 'shard', axis=0, tiled=True)  86.7 us
    all_gather x1, waiting for transfers between devices, per_device(): lax.all_gather(send_rows, 'expert', axis=0, tiled=True)  35 us
    unnamed x2, blocking collectives  29.2 us
  transfers between devices with their start and end apart: 4, of which 4 were waited for; matrix products, arithmetic and copies ran while one was open for 1% of the time, Pallas kernels for 0%

profile of v1, /device:TPU:1, one launch (start us, length us, event | category | flops | bytes accessed | tf_op | source)
XLA Modules:
  0.0 578.9 jit_solution(14014285429382318275)
XLA Ops:
  7.2 0.0 copy-start
  7.2 0.0 copy-start.7
  7.2 0.0 copy-start.5
  7.2 0.0 copy-start.3
  7.2 0.0 copy-start.6
  7.2 0.0 copy-start.8
  7.2 0.0 all-gather.3.cloned.1.call-start
  7.3 0.8 fusion.24
  8.1 0.1 copy.26
  8.2 0.2 reduce-window.4
  8.4 0.1 fusion.6
  8.5 2.0 convolution_convert_fusion.1
  10.6 0.0 all-gather.3.cloned.1.call-update
  10.6 0.0 all-gather.5.cloned.1.call-start
  10.6 0.7 convert_element_type.90
  11.3 0.0 copy-done.3
  11.3 0.8 fusion.4
  12.2 0.0 all-gather.5.cloned.1.call-update
  12.2 0.0 all-reduce.7.cloned.1.call-start
  12.3 0.0 copy-done.7
  12.3 0.6 fusion.25
  13.5 0.0 copy-done.5
  13.5 0.0 copy-done.6
  13.6 0.0 copy-start.4
  13.6 35.0 %all-gather.3.cloned.1.call-done = bf16[256,3072]{1,0:T(8,128)(2,1)} async-done(((bf16[32,3072]{1,0:T(8,128)(2,1)}), bf16[256,3072]{1,0:T(8,128)(2,1)}) %all-gather.3.cloned.1.call-update) | async-done | bytes 1572880 | tf_op jit(solution)/shard_map/all_gather | solution.py:51
  48.5 86.7 %all-gather.5.cloned.1.call-done = bf16[3072,1024]{1,0:T(8,128)(2,1)} async-done(((bf16[192,1024]{1,0:T(8,128)(2,1)}), bf16[3072,1024]{1,0:T(8,128)(2,1)}) %all-gather.5.cloned.1.call-update) | async-done | bytes 6291472 | tf_op jit(solution)/shard_map/all_gather | solution.py:62
  135.2 0.0 copy-done.8
  135.2 5.2 fusion.3
  140.4 0.0 copy-start.1
  140.4 14.6 %all-reduce.1 = f32[256]{0:T(256)S(1)} all-reduce(f32[256]{0:T(256)S(1)} %get-tuple-element.16), channel_id=2, replica_groups=mesh['dp'=4,'expert'=8,'shard'=16] {'expert'}, use_global_device_ids=true, to_apply=%region_4.5.clone | all-reduce | flops 256 | bytes 2048
  155.0 0.1 dynamic-slice.2
  155.1 1.2 gather_fusion
  156.3 0.0 copy-done.4
  156.3 0.4 convolution_convert_fusion
  156.8 0.0 copy-start.2
  156.8 3.0 convolution_multiply_fusion
  159.8 0.0 copy-done.2
  159.8 2.7 fusion.1
  162.4 0.0 all-reduce.7.cloned.1.call-update
  162.5 0.0 all-reduce.9.cloned.1.call-start
  162.5 339.5 %all-reduce.7.cloned.1.call-done = (f32[64,3072]{1,0:T(8,128)}, f32[64,3072]{1,0:T(8,128)}) async-done(((f32[64,3072]{1,0:T(8,128)}, f32[64,3072]{1,0:T(8,128)}), (f32[64,3072]{1,0:T(8,128)}, f32[64,3072]{1,0:T(8,128)})) %all-reduce.7.cloned.1.call-update) | async-done | bytes 1572880 | tf_op jit(solution)/shard_map/psum | solution.py:104
  502.1 0.0 all-reduce.9.cloned.1.call-update
  502.7 0.1 fusion.2
  502.9 0.2 dynamic-update-slice
  503.0 14.6 %all-reduce = bf16[256]{0:T(256)(128)(2,1)S(1)} all-reduce(bf16[256]{0:T(256)(128)(2,1)S(1)} %dynamic-update-slice), channel_id=1, replica_groups=mesh['dp'=4,'expert'=8,'shard'=16] {'expert'}, use_global_device_ids=true, to_apply=%add | all-reduce | flops 256 | bytes 1024
  517.7 0.9 fusion.5
  518.6 52.1 %all-reduce.9.cloned.1.call-done = (f32[64,3072]{1,0:T(8,128)}, f32[64,3072]{1,0:T(8,128)}) async-done(((f32[64,3072]{1,0:T(8,128)}, f32[64,3072]{1,0:T(8,128)}), (f32[64,3072]{1,0:T(8,128)}, f32[64,3072]{1,0:T(8,128)})) %all-reduce.9.cloned.1.call-update) | async-done | bytes 1572880 | tf_op jit(solution)/shard_map/psum | solution.py:104
  570.7 1.7 constant_dynamic-slice_fusion
  (12 shorter events, 0.1 us)
Async XLA Ops:
  7.2 149.6 %copy-start = (bf16[128,3072]{1,0:T(8,128)(2,1)S(1)}, bf16[128,3072]{1,0:T(8,128)(2,1)}, u32[]{:S(2)}) copy-start(bf16[128,3072]{1,0:T(8,128)(2,1)} %param.17) | copy-start | bytes 2359300
  7.2 5.1 copy-start.7
  7.2 6.3 %copy-start.5 = (s32[128,2]{0,1:T(2,128)S(1)}, s32[128,2]{0,1:T(2,128)}, u32[]{:S(2)}) copy-start(s32[128,2]{0,1:T(2,128)} %param.12) | copy-start | bytes 3076
  7.2 4.1 copy-start.3
  7.2 6.3 %copy-start.6 = (f32[128,8]{0,1:T(8,128)S(1)}, f32[128,8]{0,1:T(8,128)}, u32[]{:S(2)}) copy-start(f32[128,8]{0,1:T(8,128)} %param.11) | copy-start | bytes 12292
  7.2 128.0 %copy-start.8 = (bf16[1,1,256,1024]{3,2,1,0:T(8,128)(2,1)S(1)}, bf16[1,1,256,1024]{3,2,1,0:T(8,128)(2,1)}, u32[]{:S(2)}) copy-start(bf16[1,1,256,1024]{3,2,1,0:T(8,128)(2,1)} %param.16) | copy-start | bytes 1572868
  7.2 41.3 %all-gather.3.cloned.1.call-start = ((), (), s32[]{:S(2)}) async-start(), calls=%async_computation | async-start | bytes 1769472 | tf_op jit(solution)/shard_map/all_gather | solution.py:51
  10.6 124.6 %all-gather.5.cloned.1.call-start = ((), (), s32[]{:S(2)}) async-start(), calls=%async_computation.1 | async-start | bytes 6684672 | tf_op jit(solution)/shard_map/all_gather | solution.py:62
  12.2 489.9 %all-reduce.7.cloned.1.call-start = ((), (), s32[]{:S(2)}) async-start(), calls=%async_computation.2 | async-start | bytes 3145728 | tf_op jit(solution)/shard_map/psum | solution.py:104
  13.6 142.8 %copy-start.4 = (bf16[8,3072]{1,0:T(8,128)(2,1)S(1)}, bf16[8,3072]{1,0:T(8,128)(2,1)}, u32[]{:S(2)}) copy-start(bf16[8,3072]{1,0:T(8,128)(2,1)} %param.13) | copy-start | bytes 147460
  140.4 16.4 %copy-start.1 = (bf16[128,3072]{1,0:T(8,128)(2,1)S(1)}, bf16[128,3072]{1,0:T(8,128)(2,1)}, u32[]{:S(2)}) copy-start(bf16[128,3072]{1,0:T(8,128)(2,1)} %param.10) | copy-start | bytes 2359300
  156.8 3.0 copy-start.2
  162.5 408.2 %all-reduce.9.cloned.1.call-start = ((), (), s32[]{:S(2)}) async-start(), calls=%async_computation.3 | async-start | bytes 3145728 | tf_op jit(solution)/shard_map/psum | solution.py:104
Sparse Core Ops, SparseCore 0:
  10.8 37.7 all-gather.2
  51.2 83.9 all-gather.4
  162.6 339.4 all-reduce.6
  504.4 66.2 all-reduce.8
